TPU v7x, 128 devices: a whole 4x4x4 slice. The times are simulated.
128 devices in a mesh: row: 16 (over x, z), col: 8 (over y, core).
Axes of the slice: x: 4, y: 4, z: 4, core: 2. Of those that a mesh axis runs over, the one named last changes fastest.
Arguments:
- momentum: float32 [12288, 16384], P('row', 'col')
- gradient: bfloat16 [12288, 16384], P('row', 'col'), may hold values from -4 to 4
- factor: float32 [16384, 512], P('col'), may hold values from -6 to 6
- serve_perm: int32 [96], replicated, may hold values from 0 to 95, as said below
Outputs:
- new_momentum: float32 [12288, 16384], P('row', 'col')
- new_factor: float32 [16384, 512], P('col')
- served: float32 [12288, 16384], P('row', 'col')
Inputs may be any that keep to these rules, and one draw needn't show every extreme that they name: `serve_perm`: A permutation of the 96 blocks. Serving blocks at even positions within a device's 6 blocks come from the first half of the rows (gate), odd ones from the second half (up). The blocks that stand on one index of row go to 6 different indices of row, and each index of row receives from 6 different ones.
All inputs are finite; a program needn't handle non-finite values.
Results may differ from a plain program's by a relative error of at most 0.0003.
Values sent between devices are 32-bit elements; how exact they have to be, the bound alone decides.
A program may use at most 192 MiB of HBM per device.

v0:
```python
import jax
import jax.numpy as jnp
from jax import lax
from jax.sharding import PartitionSpec as P

N = 16384


learn_rate = 0.01


def mult(left, right):
    return jnp.dot(left, right, precision=lax.Precision.HIGHEST, preferred_element_type=jnp.float32)


def outgoing(values, serve_perm, n_row):
    block_count = values.shape[0] // 128
    blocks = values.reshape(block_count, 128, values.shape[1])
    mine = lax.axis_index("row") * block_count + jnp.arange(block_count, dtype=jnp.int32)
    places = jnp.arange(serve_perm.shape[0], dtype=jnp.int32)
    position = jnp.sum(jnp.where(serve_perm[None, :] == mine[:, None], places[None, :], 0), axis=1)
    target = position // block_count
    onehot = (target[None, :] == jnp.arange(n_row, dtype=jnp.int32)[:, None]).astype(jnp.float32)
    sendbuf = jnp.einsum("el,lrc->erc", onehot, blocks, precision=lax.Precision.HIGHEST)
    return sendbuf.reshape(n_row * 128, values.shape[1])


def incoming(received, serve_perm, n_row, block_count):
    mine = lax.axis_index("row") * block_count + jnp.arange(block_count, dtype=jnp.int32)
    sources = serve_perm[mine] // block_count
    onehot = (sources[:, None] == jnp.arange(n_row, dtype=jnp.int32)[None, :]).astype(jnp.float32)
    pieces = received.reshape(n_row, 128, received.shape[1])
    placed = jnp.einsum("te,erc->trc", onehot, pieces, precision=lax.Precision.HIGHEST)
    return placed.reshape(block_count * 128, received.shape[1])


def body(momentum, gradient, factor, serve_perm):
    n_row = lax.axis_size("row")
    rows_dev = momentum.shape[0]
    block_count = rows_dev // 128
    buffer = momentum + gradient.astype(jnp.float32)
    power = lax.psum(mult(buffer, factor), "col")
    gram = lax.psum(mult(power.T, power), "row")
    lower = jnp.linalg.cholesky(gram)
    ortho = lax.linalg.triangular_solve(lower, power, left_side=False, lower=True, transpose_a=True)
    right = lax.psum(mult(buffer.T, ortho), "row")
    colsq = lax.psum(jnp.sum(right * right, axis=0), "col")
    new_momentum = buffer - 0.05 * mult(ortho, right.T)
    new_factor = right / jnp.sqrt(colsq + 1e-06)
    coefficient = jnp.float32(learn_rate) * jnp.sqrt(jnp.float32(rows_dev * n_row) / jnp.float32(N))
    update = -coefficient * mult(ortho, new_factor.T)
    moved = lax.all_to_all(
        outgoing(update, serve_perm, n_row), "row", split_axis=0, concat_axis=0, tiled=True
    )
    served = incoming(moved, serve_perm, n_row, block_count)
    return (new_momentum, new_factor, served)


def solution(mesh):
    return jax.shard_map(
        body,
        mesh=mesh,
        in_specs=(P("row", "col"), P("row", "col"), P("col", None), P()),
        out_specs=(P("row", "col"), P("col", None), P("row", "col")),
        check_vma=False,
    )
```

profile of v0, /device:TPU:125, one launch (start us, length us, event | category | flops | bytes accessed | tf_op | source)
XLA Modules:
  0.0 884.8 jit_solution(12843369326498280776)
XLA Ops:
  7.2 14.6 %fusion.5 = f32[768,512]{1,0:T(8,128)} fusion(f32[2048,512]{1,0:T(8,128)} %param.6, f32[768,2048]{1,0:T(8,128)} %param.4, bf16[768,2048]{1,0:T(8,128)(2,1)} %param.5), kind=kOutput, calls=%fused_computation.12 | convolution fusion | flops 9666822144 | bytes 15204352 | tf_op jit(solution)/shard_map/dot_general | solution.py:13
  21.8 64.1 %all-reduce.5.cloned.1.call-done = f32[768,512]{1,0:T(8,128)} async-done(((f32[768,512]{1,0:T(8,128)}), f32[768,512]{1,0:T(8,128)}) %all-reduce.5.cloned.1.call-update) | async-done | bytes 1572880 | tf_op jit(solution)/shard_map/psum | solution.py:42
  85.9 5.6 fusion.47
  91.8 83.9 %all-reduce.7.cloned.1.call-done = f32[512,512]{0,1:T(8,128)} async-done(((f32[512,512]{0,1:T(8,128)}), f32[512,512]{0,1:T(8,128)}) %all-reduce.7.cloned.1.call-update) | async-done | bytes 1048592 | tf_op jit(solution)/shard_map/psum | solution.py:43
  175.7 1.6 copy.19
  177.3 1.4 fusion.11
  178.7 11.7 %cholesky.104 = f32[128,128]{1,0:T(8,128)S(1)} custom-call(f32[128,128]{1,0:T(8,128)S(1)} %cholesky.266), custom_call_target="Cholesky" | custom-call | tf_op jit(solution)/shard_map/jit(cholesky)/cholesky | solution.py:44
  190.5 9.8 %custom-call.30 = f32[1,128,128]{1,2,0:T(8,128)S(1)} custom-call(f32[1,128,128]{2,1,0:T(8,128)S(1)} %get-tuple-element.30), custom_call_target="InvertDiagBlocksLowerTriangular" | custom-call | tf_op jit(solution)/shard_map/jit(cholesky)/cholesky | solution.py:44
  201.1 11.7 %cholesky.217 = f32[128,128]{1,0:T(8,128)S(1)} custom-call(f32[128,128]{1,0:T(8,128)S(1)} %cholesky.270), custom_call_target="Cholesky" | custom-call | tf_op jit(solution)/shard_map/jit(cholesky)/cholesky | solution.py:44
  212.9 10.0 %custom-call.31 = f32[1,128,128]{1,2,0:T(8,128)S(1)} custom-call(f32[1,128,128]{2,1,0:T(8,128)S(1)} %get-tuple-element.27), custom_call_target="InvertDiagBlocksLowerTriangular" | custom-call | tf_op jit(solution)/shard_map/jit(cholesky)/cholesky | solution.py:44
  223.2 1.4 convolution_subtract_fusion.4
  224.6 11.7 %cholesky.238 = f32[128,128]{1,0:T(8,128)S(1)} custom-call(f32[128,128]{1,0:T(8,128)S(1)} %cholesky.275), custom_call_target="Cholesky" | custom-call | tf_op jit(solution)/shard_map/jit(cholesky)/cholesky | solution.py:44
  236.4 0.7 compare_reduce_fusion.1
  237.0 9.8 %custom-call.32 = f32[1,128,128]{1,2,0:T(8,128)S(1)} custom-call(f32[1,128,128]{2,1,0:T(8,128)S(1)} %get-tuple-element.24), custom_call_target="InvertDiagBlocksLowerTriangular" | custom-call | tf_op jit(solution)/shard_map/jit(cholesky)/cholesky | solution.py:44
  247.0 1.2 convolution_subtract_fusion.5
  248.3 11.7 %cholesky.255 = f32[128,128]{1,0:T(8,128)S(1)} custom-call(f32[128,128]{1,0:T(8,128)S(1)} %convolution_subtract_fusion.5), custom_call_target="Cholesky" | custom-call | tf_op jit(solution)/shard_map/jit(cholesky)/cholesky | solution.py:44
  260.0 0.7 compare_reduce_fusion
  260.7 0.7 compare_reduce_fusion.2
  263.9 1.5 select_select_fusion
  265.4 14.1 %while.1 = (s32[]{:T(128)}, f32[512,512]{1,0:T(8,128)}, s32[4,2]{0,1:T(2,128)S(1)}, f32[4,128,128]{2,1,0:T(8,128)}, s32[]{:T(128)}) while((s32[]{:T(128)}, f32[512,512]{1,0:T(8,128)}, s32[4,2]{0,1:T(2,128)S(1)}, f32[4,128,128]{2,1,0:T(8,128)}, s32[]{:T(128)}) %tuple.31), condition=%wide.while_cond, body=%wide.while_body.sunk | while | flops 2 | bytes 132705 | solution.py:45
  265.5 0.6 fusion.59
  266.1 2.9 bitcast_dynamic-update-slice_fusion.2
  269.0 0.6 fusion.59
  269.6 2.9 bitcast_dynamic-update-slice_fusion.2
  272.6 0.6 fusion.59
  273.1 2.9 bitcast_dynamic-update-slice_fusion.2
  276.7 2.8 bitcast_dynamic-update-slice_fusion.2
  279.5 40.1 %custom-call.33 = f32[4,128,128]{1,2,0:T(8,128)S(1)} custom-call(f32[4,128,128]{2,1,0:T(8,128)} %get-tuple-element.10), custom_call_target="InvertDiagBlocksLowerTriangular" | custom-call | tf_op jit(solution)/shard_map/triangular_solve | solution.py:45
  319.6 1.7 fusion.15
  321.3 2.0 convolution_subtract_fusion.1
  323.8 2.6 convolution_subtract_fusion.2
  327.0 3.3 convolution_subtract_fusion
  330.9 0.7 copy-done.6
  331.6 21.4 %fusion.4 = f32[2048,512]{1,0:T(8,128)} fusion(f32[768,2048]{1,0:T(8,128)S(1)} %bitcast.65, bf16[768,2048]{1,0:T(8,128)(2,1)S(1)} %copy-done.1, f32[768,128]{0,1:T(8,128)S(1)} %fusion.25, f32[768,128]{0,1:T(8,128)S(1)} %fusion.26, f32[768,128]{0,1:T(8,128)S(1)} %fusion.27, f32[768,128]{0,1:T(8,128)S(1)} %fusion.15), kind=kOutput, calls=%fused_computation.11 | convolution fusion | flops 9668001792 | bytes 15204352 | tf_op jit(solution)/shard_map/dot_general | solution.py:13
  353.1 0.6 copy-done
  353.9 103.8 %all-reduce.9.cloned.1.call-done = f32[2048,512]{1,0:T(8,128)} async-done(((f32[2048,512]{1,0:T(8,128)}), f32[2048,512]{1,0:T(8,128)}) %all-reduce.9.cloned.1.call-update) | async-done | bytes 4194320 | tf_op jit(solution)/shard_map/psum | solution.py:46
  457.7 2.5 multiply_reduce_fusion
  460.2 12.1 %psum.31 = f32[512]{0:T(512)S(1)} all-reduce(f32[512]{0:T(512)S(1)} %multiply_reduce_fusion), channel_id=1, replica_groups=mesh['row'=16,'col'=8] {'col'}, use_global_device_ids=true, to_apply=%region_12.13 | all-reduce | flops 512 | bytes 4096 | tf_op jit(solution)/shard_map/psum | solution.py:47
  472.3 2.8 broadcast_divide_fusion
  475.1 20.4 %convolution_multiply_fusion = f32[768,2048]{1,0:T(8,128)S(1)} fusion(f32[2048,512]{1,0:T(8,128)S(1)} %broadcast_divide_fusion, f32[768,128]{0,1:T(8,128)S(1)} %copy-done.7, f32[768,128]{0,1:T(8,128)S(1)} %fusion.26, f32[768,128]{0,1:T(8,128)S(1)} %fusion.27, f32[768,128]{0,1:T(8,128)S(1)} %fusion.15), kind=kOutput, calls=%fused_computation.10 | convolution fusion | flops 9666428928 | bytes 12058624 | tf_op jit(solution)/shard_map/dot_general | solution.py:13
  495.6 11.5 %fusion.2 = f32[16,128,2048]{2,0,1:T(8,128)S(1)} fusion(f32[6,128,2048]{2,1,0:T(8,128)S(1)} %bitcast.63, s32[6]{0:T(128)S(1)} %and_select_fusion), kind=kOutput, calls=%fused_computation.5 | convolution fusion | flops 301989984 | bytes 23068696 | tf_op jit(solution)/shard_map/el,lrc->erc/dot_general | solution.py:24
  507.1 18.4 %copy.21 = f32[16,128,2048]{2,1,0:T(8,128)} copy(f32[16,128,2048]{2,0,1:T(8,128)S(1)} %fusion.2) | data formatting | bytes 33554432 | tf_op jit(solution)/shard_map/el,lrc->erc/dot_general | solution.py:24
  525.5 7.4 all-to-all-start
  532.9 0.6 gather_fusion
  533.6 24.8 %multiply_subtract_fusion = f32[768,2048]{1,0:T(8,128)} fusion(f32[2048,512]{1,0:T(8,128)} %all-reduce.9.cloned.1.call-done, f32[768,2048]{1,0:T(8,128)} %param.4, bf16[768,2048]{1,0:T(8,128)(2,1)S(1)} %copy-done.2, f32[768,128]{0,1:T(8,128)} %copy-done.6, f32[768,128]{0,1:T(8,128)} %copy-done.5, f32[768,128]{0,1:T(8,128)} %copy-done.4, ...), kind=kOutput, calls=%fused_computation.7 | convolution fusion | flops 9671147520 | bytes 21495808 | tf_op jit(solution)/shard_map/dot_general | solution.py:13
  558.4 291.7 %all-to-all-done = f32[16,128,2048]{2,1,0:T(8,128)} async-done(((f32[16,128,2048]{2,1,0:T(8,128)}), f32[16,128,2048]{2,1,0:T(8,128)}, u32[]{:S(2)}, u32[]{:S(2)}) %all-to-all-start) | async-done | bytes 16777248 | tf_op jit(solution)/shard_map/all_to_all | solution.py:52
  850.0 21.4 %fusion = f32[6,128,2048]{2,0,1:T(8,128)S(1)} fusion(f32[16,128,2048]{2,1,0:T(8,128)} %all-to-all-done, s32[6]{0:T(128)S(1)} %and_select_fusion.1), kind=kOutput, calls=%fused_computation.3 | convolution fusion | flops 301989984 | bytes 23068696 | tf_op jit(solution)/shard_map/te,erc->trc/dot_general | solution.py:33
  871.4 6.3 copy.23
  (57 shorter events, 4.5 us)
Async XLA Ops:
  7.2 78.8 %all-reduce.5.cloned.1.call-start = ((), (), s32[]{:S(2)}) async-start(), calls=%async_computation.1 | async-start | bytes 3145728 | tf_op jit(solution)/shard_map/psum | solution.py:42
  21.8 153.9 %all-reduce.7.cloned.1.call-start = ((), (), s32[]{:S(2)}) async-start(), calls=%async_computation.2 | async-start | bytes 2097152 | tf_op jit(solution)/shard_map/psum | solution.py:43
  91.5 366.1 %all-reduce.9.cloned.1.call-start = ((), (), s32[]{:S(2)}) async-start(), calls=%async_computation.3 | async-start | bytes 8388608 | tf_op jit(solution)/shard_map/psum | solution.py:46
  178.7 44.1 %copy-start.8 = (f32[512,512]{1,0:T(8,128)}, f32[512,512]{1,0:T(8,128)S(1)}, u32[]{:S(2)}) copy-start(f32[512,512]{1,0:T(8,128)S(1)} %fusion.11) | copy-start | bytes 3145732
  223.1 108.5 %slice-start = ((s8[6291456]{0:T(1024)(128)(4,1)}), s8[2097152]{0:T(1024)(128)(4,1)S(1)}, s32[]{:S(2)}) async-start(s8[6291456]{0:T(1024)(128)(4,1)} %bitcast.64), calls=%async_computation.4 | async-start | bytes 4194304
  319.6 12.0 %copy-start.1 = (bf16[768,2048]{1,0:T(8,128)(2,1)S(1)}, bf16[768,2048]{1,0:T(8,128)(2,1)}, u32[]{:S(2)}) copy-start(bf16[768,2048]{1,0:T(8,128)(2,1)} %param.5) | copy-start | bytes 9437188
  321.3 10.3 %slice-start.1 = ((s8[6291456]{0:T(1024)(128)(4,1)}), s8[4194304]{0:T(1024)(128)(4,1)S(1)}, s32[]{:S(2)}) async-start(s8[6291456]{0:T(1024)(128)(4,1)} %bitcast.64), calls=%async_computation.5 | async-start | bytes 8388608
  323.8 151.2 %copy-start.4 = (f32[768,128]{0,1:T(8,128)}, f32[768,128]{0,1:T(8,128)S(1)}, u32[]{:S(2)}) copy-start(f32[768,128]{0,1:T(8,128)S(1)} %fusion.27) | copy-start | bytes 1179652
  327.0 148.1 %copy-start.5 = (f32[768,128]{0,1:T(8,128)}, f32[768,128]{0,1:T(8,128)S(1)}, u32[]{:S(2)}) copy-start(f32[768,128]{0,1:T(8,128)S(1)} %fusion.26) | copy-start | bytes 1179652
  330.9 0.7 copy-start.6
  353.0 0.7 copy-start
  472.3 2.8 copy-start.7
  475.1 20.5 %copy-start.3 = (f32[2048,512]{1,0:T(8,128)}, f32[2048,512]{1,0:T(8,128)S(1)}, u32[]{:S(2)}) copy-start(f32[2048,512]{1,0:T(8,128)S(1)} %broadcast_divide_fusion) | copy-start | bytes 12582916
  525.5 8.1 copy-start.2
  525.5 324.6 %all-to-all-start = ((f32[16,128,2048]{2,1,0:T(8,128)}), f32[16,128,2048]{2,1,0:T(8,128)}, u32[]{:S(2)}, u32[]{:S(2)}) async-start(f32[16,128,2048]{2,1,0:T(8,128)} %copy.21), calls=%async_computation | async-start | bytes 33554432 | tf_op jit(solution)/shard_map/all_to_all | solution.py:52
Sparse Core Ops, SparseCore 0:
  21.9 63.9 all-reduce.4
  91.6 84.0 all-reduce.6
  353.2 104.4 all-reduce.8
where the time goes:
time: 891 us; the launch traced here: 885 us
  waiting for transfers between devices  544 us (61%)
  matrix products  135 us (15%)
  other arithmetic  127 us (14%)
  local copies, waits for them, and re-layouts  42.5 us (5%)
  between operations  17.2 us (2%)
  blocking collectives  12.1 us (1%)
    all_to_all x1, waiting for transfers between devices, body(): lax.all_to_all(outgoing(update, serve_perm, n_row), 'row', split_axis=0,...  292 us
    psum x1, waiting for transfers between devices, body(): right = lax.psum(mult(buffer.T, ortho), 'row')  104 us
    dot_general x5, matrix products, mult(): jnp.dot(left, right, precision=lax.Precision.HIGHEST, preferred_element_t...  86.8 us
    psum x1, waiting for transfers between devices, body(): gram = lax.psum(mult(power.T, power), 'row')  83.9 us
    another operation x14, other arithmetic, body(): lower = jnp.linalg.cholesky(gram)  78.6 us
    psum x1, waiting for transfers between devices, body(): power = lax.psum(mult(buffer, factor), 'col')  64.1 us
    another operation x3, other arithmetic, body(): lax.linalg.triangular_solve(lower, power, left_side=False, lower=True, tr...  41.6 us
    dot_general x1, matrix products, incoming(): jnp.einsum('te,erc->trc', onehot, pieces, precision=lax.Precision.HIGHEST)  21.4 us
  transfers between devices with their start and end apart: 4, of which 4 were waited for; matrix products, arithmetic and copies ran while one was open for 3% of the time, Pallas kernels for 0%

commit v1 on v0

v1 whole, which is shorter than its diff:
```python
import jax
import jax.numpy as jnp
from jax import lax
from jax.experimental import pallas as pl
from jax.experimental.pallas import tpu as pltpu
from jax.sharding import PartitionSpec as P

N = 16384
ROWS = 12288
RANK = 512
learn_rate = 0.01

f32 = jnp.float32
bf16 = jnp.bfloat16
HIGHEST = lax.Precision.HIGHEST
MESH = pl.DeviceIdType.MESH
NN = (((1,), (0,)), ((), ()))
NT = (((1,), (1,)), ((), ()))


def mm(a, b, dims=NN):
    return lax.dot_general(a, b, dims, preferred_element_type=f32)


def mm_exact(a, b, dims=NN):
    return lax.dot_general(a, b, dims, precision=HIGHEST, preferred_element_type=f32)


def split(a):
    high = a.astype(bf16)
    return high, (a - high.astype(f32)).astype(bf16)


def eliminate(block):
    lane = lax.broadcasted_iota(jnp.int32, (8, 128), 1)
    sub = lax.broadcasted_iota(jnp.int32, (8, 128), 0)
    done = []
    rest = block
    for first in range(0, 128, 8):
        height = 128 - first
        cols = [jnp.broadcast_to(rest[:, first + j:first + j + 1], (height, 128)) for j in range(8)]
        inside = (lane >= first) & (lane < first + 8)
        tile = jnp.where(inside, 0.0, rest[:8])
        factors, rows = [], []
        for i in range(8):
            scale = lax.rsqrt(jnp.broadcast_to(cols[i][i:i + 1], (8, 128)))
            column = cols[i] * scale[:1]
            factors.append(column)
            for j in range(i + 1, 8):
                cols[j] = cols[j] - column * column[j:j + 1]
            row = jnp.broadcast_to(jnp.where(lane == first + i, 1.0, tile)[i:i + 1], (8, 128)) * scale
            rows.append(row)
            tile = jnp.where(sub > i, tile - column[:8] * row, jnp.where(sub == i, row, tile))
        done.append(tile)
        if height > 8:
            wide = lax.broadcasted_iota(jnp.int32, (height - 8, 128), 1)
            rest = jnp.where((wide >= first) & (wide < first + 8), 0.0, rest[8:])
            for i in range(8):
                rest = rest - factors[i][8:] * rows[i][:1]
    return jnp.concatenate(done, axis=0)


def fused(perm_ref, mom_hbm, grad_hbm, fac_hbm,
          rt_hi, rt_lo, ortho_out, oph_out, opl_out, scale_out,
          mom, grad, fac, buf_hi, buf_lo, fac_hi, fac_lo, part, from_core, to_y, from_y,
          power, pt_hi, pt_lo, gpart, gfrom, gram, work, zt, zfrom1, zsum1, zfrom2, zo,
          psend, pfrom, ppiece, pperm, csq, cfrom,
          lsem, a1s, a1r, a2s, a2r, bs, br, b2s, b2r, g1s, g1r, g2s, g2r, g3s, g3r, g4s, g4r,
          z1s, z1r, z2s, z2r, z3s, z3r, z4s, z4r, p1s, p1r, p2s, p2r, cs, cr):
    me_row = lax.axis_index("row")
    me_col = lax.axis_index("col")
    x, z = me_row // 4, me_row % 4
    y, core = me_col // 2, me_col % 2
    mate = (me_row, y * 2 + 1 - core)
    pending = []

    def send(src, dst, ssem, rsem, dev):
        copy = pltpu.make_async_remote_copy(src_ref=src, dst_ref=dst, send_sem=ssem, recv_sem=rsem,
                                            device_id=dev, device_id_type=MESH)
        copy.start()
        pending.append(copy)

    def arrive(dst, ssem, rsem):
        pltpu.make_async_remote_copy(src_ref=dst, dst_ref=dst, send_sem=ssem, recv_sem=rsem,
                                     device_id=mate, device_id_type=MESH).wait_recv()

    other = pl.multiple_of((1 - core) * 384, 384)
    mine = pl.multiple_of(core * 384, 384)

    loads = [pltpu.make_async_copy(fac_hbm, fac, lsem.at[0])]
    for h, start in enumerate((other, mine)):
        rows = pl.ds(start, 384)
        loads.append(pltpu.make_async_copy(mom_hbm.at[rows], mom.at[rows], lsem.at[1 + 2 * h]))
        loads.append(pltpu.make_async_copy(grad_hbm.at[rows], grad.at[rows], lsem.at[2 + 2 * h]))
    for copy in loads:
        copy.start()

    barrier = pltpu.get_barrier_semaphore()
    for d in range(1, 16):
        pl.semaphore_signal(barrier, inc=1, device_id=((me_row + d) % 16, me_col), device_id_type=MESH)
    for d in range(1, 8):
        pl.semaphore_signal(barrier, inc=1, device_id=(me_row, (me_col + d) % 8), device_id_type=MESH)

    loads[0].wait()

    @pl.loop(0, 32)
    def _(i):
        rows = pl.ds(pl.multiple_of(i * 64, 64), 64)
        high, low = split(fac[rows, :])
        fac_hi[rows, :] = high
        fac_lo[rows, :] = low

    def power_half(h, start):
        loads[1 + 2 * h].wait()
        loads[2 + 2 * h].wait()

        @pl.loop(0, 12)
        def _(i):
            rows = pl.ds(pl.multiple_of(start + i * 32, 32), 32)
            high, low = split(mom[rows, :] + grad[rows, :].astype(f32))
            buf_hi[rows, :] = high
            buf_lo[rows, :] = low

        rows = pl.ds(start, 384)
        part[rows, :] = (mm(buf_hi[rows, :], fac_hi[...]) + mm(buf_hi[rows, :], fac_lo[...])
                         + mm(buf_lo[rows, :], fac_hi[...]))

    power_half(0, other)
    pl.semaphore_wait(barrier, 22)
    for d in (2, 1, 3, 0):
        to = (y + d) % 4
        send(part.at[pl.ds(pl.multiple_of(other + to * 96, 96), 96)], from_core.at[to],
             a1s.at[d], a1r.at[to], mate)
    power_half(1, mine)
    for d in (2, 1, 3):
        to = (y + d) % 4
        arrive(from_core.at[to], a1s.at[d], a1r.at[to])
        to_y[to] = part[pl.ds(pl.multiple_of(mine + to * 96, 96), 96), :] + from_core[to]
        send(to_y.at[to], from_y.at[y], a2s.at[d], a2r.at[y], (me_row, to * 2 + core))
    arrive(from_core.at[y], a1s.at[0], a1r.at[y])
    own = part[pl.ds(pl.multiple_of(mine + y * 96, 96), 96), :] + from_core[y]
    for d in (1, 3, 2):
        src = (y + d) % 4
        arrive(from_y.at[src], a2s.at[d], a2r.at[src])
        own = own + from_y[src]
    here = pl.ds(pl.multiple_of(mine + y * 96, 96), 96)
    power[here, :] = own
    for d in (2, 1, 3):
        to = (y + d) % 4
        send(power.at[here], power.at[here], bs.at[d], br.at[y], (me_row, to * 2 + core))
    send(power.at[here], power.at[here], b2s.at[0], b2r.at[y], mate)
    for d in (1, 3, 2):
        src = (y + d) % 4
        there = pl.ds(pl.multiple_of(mine + src * 96, 96), 96)
        arrive(power.at[there], bs.at[d], br.at[src])
        send(power.at[there], power.at[there], b2s.at[d], b2r.at[src], mate)
    for d in (0, 1, 3, 2):
        src = (y + d) % 4
        there = pl.ds(pl.multiple_of(other + src * 96, 96), 96)
        arrive(power.at[there], b2s.at[d], b2r.at[src])

    for j in range(6):
        high, low = split(power[j * 128:j * 128 + 128, :].T)
        pt_hi[:, j * 128:j * 128 + 128] = high
        pt_lo[:, j * 128:j * 128 + 128] = low

    strip = pl.ds(pl.multiple_of(me_col * 64, 64), 64)
    p_hi, p_lo = pt_hi[strip, :], pt_lo[strip, :]
    gpart[...] = (mm(p_hi, pt_hi[...], NT) + mm(p_hi, pt_lo[...], NT)
                  + mm(p_lo, pt_hi[...], NT) + mm(p_lo, pt_lo[...], NT))

    def unit(r, base=0):
        return (pl.ds(pl.multiple_of(base + (r // 2) * 8, 8), 8), pl.ds(pl.multiple_of((r % 2) * 256, 256), 256))

    for d in range(1, 16):
        to = (me_row + d) % 16
        send(gpart.at[unit(to)], gfrom.at[me_row], g1s.at[d], g1r.at[me_row], (to, me_col))

    def pick(dest):
        local = jnp.int32(0)
        for t in range(6):
            b = perm_ref[dest * 6 + t] - me_row * 6
            local = local + jnp.where((b >= 0) & (b < 6), b, 0)
        share = power[pl.ds(pl.multiple_of(me_col * 16, 16), 16), :]
        for l in range(1, 6):
            share = jnp.where(local == l, power[pl.ds(pl.multiple_of(l * 128 + me_col * 16, 16), 16), :], share)
        return share

    for d in range(1, 16):
        to = (me_row + d) % 16
        psend[d] = pick(to)
    pfrom[me_row] = pick(me_row)

    def z_half(h):
        @pl.loop(0, 2)
        def _(t):
            cols = pl.ds(pl.multiple_of(h * 1024 + t * 512, 512), 512)
            zt[h, :, pl.ds(pl.multiple_of(t * 512, 512), 512)] = (
                mm(pt_hi[...], buf_hi[:, cols]) + mm(pt_hi[...], buf_lo[:, cols])
                + mm(pt_lo[...], buf_hi[:, cols]))

    z_half(0)
    total = gpart[unit(me_row)]
    for d in range(1, 16):
        src = (me_row + d) % 16
        arrive(gfrom.at[src], g1s.at[d], g1r.at[src])
        total = total + gfrom[src]
    gram[unit(me_row, me_col * 64)] = total
    for d in range(1, 16):
        to = (me_row + d) % 16
        piece = gram.at[unit(me_row, me_col * 64)]
        send(piece, piece, g2s.at[d], g2r.at[me_row], (to, me_col))
    z_half(1)
    for d in range(1, 16):
        src = (me_row + d) % 16
        arrive(gram.at[unit(src, me_col * 64)], g2s.at[d], g2r.at[src])

    def strip_of(c):
        return pl.ds(pl.multiple_of(c * 64, 64), 64)

    for d in (2, 1, 3):
        to = (y + d) % 4
        send(gram.at[strip], gram.at[strip], g3s.at[d], g3r.at[y], (me_row, to * 2 + core))
    send(gram.at[strip], gram.at[strip], g4s.at[0], g4r.at[y], mate)

    axes = ((x, z), (z, x))

    def peer(h, level, to):
        along_x = (h == 0) == (level == 0)
        return (to * 4 + z, me_col) if along_x else (x * 4 + to, me_col)

    for d in (2, 1, 3):
        for h in range(2):
            a, b = axes[h]
            to = (a + d) % 4
            send(zt.at[h, pl.ds(pl.multiple_of(to * 128, 128), 128)], zfrom1.at[h, a],
                 z1s.at[h, d], z1r.at[h, a], peer(h, 0, to))
    for d in range(1, 16):
        to = (me_row + d) % 16
        send(psend.at[d], pfrom.at[me_row], p1s.at[d], p1r.at[me_row], (to, me_col))

    for d in (1, 3, 2):
        src = (y + d) % 4
        there = strip_of(src * 2 + core)
        arrive(gram.at[there], g3s.at[d], g3r.at[src])
        send(gram.at[there], gram.at[there], g4s.at[d], g4r.at[src], mate)
    for d in (0, 1, 3, 2):
        src = (y + d) % 4
        arrive(gram.at[strip_of(src * 2 + 1 - core)], g4s.at[d], g4r.at[src])

    def z_second():
        for h in range(2):
            a, b = axes[h]
            total = zt[h, pl.ds(pl.multiple_of(a * 128, 128), 128), :]
            for d in (1, 3, 2):
                src = (a + d) % 4
                arrive(zfrom1.at[h, src], z1s.at[h, d], z1r.at[h, src])
                total = total + zfrom1[h, src]
            zsum1[h] = total
            for d in (2, 1, 3):
                to = (b + d) % 4
                send(zsum1.at[h, pl.ds(pl.multiple_of(to * 32, 32), 32)], zfrom2.at[h, b],
                     z2s.at[h, d], z2r.at[h, b], peer(h, 1, to))

    def place(h, b):
        return pl.ds(pl.multiple_of(axes[h][0] * 128 + b * 32, 32), 32)

    def z_third():
        for h in range(2):
            a, b = axes[h]
            total = zsum1[h, pl.ds(pl.multiple_of(b * 32, 32), 32), :]
            for d in (1, 3, 2):
                src = (b + d) % 4
                arrive(zfrom2.at[h, src], z2s.at[h, d], z2r.at[h, src])
                total = total + zfrom2[h, src]
            zo[h, place(h, b), :] = total
            for d in (2, 1, 3):
                to = (b + d) % 4
                piece = zo.at[h, place(h, b)]
                send(piece, piece, z3s.at[h, d], z3r.at[h, b], peer(h, 1, to))

    def z_fourth():
        for h in range(2):
            a, b = axes[h]
            for d in (1, 3, 2):
                src = (b + d) % 4
                arrive(zo.at[h, place(h, src)], z3s.at[h, d], z3r.at[h, src])
            piece = zo.at[h, pl.ds(pl.multiple_of(a * 128, 128), 128)]
            for d in (2, 1, 3):
                to = (a + d) % 4
                send(piece, piece, z4s.at[h, d], z4r.at[h, a], peer(h, 0, to))

    def perm_second():
        for t in range(6):
            first = perm_ref[me_row * 6 + t]
            share = pfrom[0]
            for r in range(1, 16):
                share = jnp.where(first >= r * 6, pfrom[r], share)
            ppiece[t] = share
        mine_rows = pl.ds(pl.multiple_of(me_col * 16, 16), 16)
        pperm[:, mine_rows, :] = ppiece[...]
        for d in range(1, 8):
            to = (me_col + d) % 8
            send(ppiece, pperm.at[:, mine_rows], p2s.at[d], p2r.at[me_col], (me_row, to))

    li = lax.broadcasted_iota(jnp.int32, (128, 128), 0)
    lj = lax.broadcasted_iota(jnp.int32, (128, 128), 1)

    work[...] = gram[...]
    for k in range(4):
        s = slice(128 * k, 128 * k + 128)
        inv = jnp.where(li >= lj, eliminate(work[s, s]), 0.0)
        work[s, s] = jnp.where(li == lj, 1.0, 0.0)
        row = mm_exact(inv, work[s, :])
        work[s, :] = row
        if k < 3:
            r = slice(128 * k + 128, 512)
            low = mm_exact(work[r, s], inv, NT)
            work[r, s] = jnp.zeros((512 - 128 * k - 128, 128), f32)
            work[r, :] = work[r, :] - mm_exact(low, row)
        if k == 0:
            for d in range(1, 16):
                src = (me_row + d) % 16
                arrive(pfrom.at[src], p1s.at[d], p1r.at[src])
            perm_second()
        if k == 1:
            z_second()
        if k == 2:
            z_third()
        if k == 3:
            z_fourth()

    ii = lax.broadcasted_iota(jnp.int32, (512, 512), 0)
    jj = lax.broadcasted_iota(jnp.int32, (512, 512), 1)
    inv_hi, inv_lo = split(jnp.where(ii >= jj, work[...], 0.0))

    def times_inverse(block):
        high, low = split(block)
        return mm(high, inv_hi, NT) + mm(high, inv_lo, NT) + mm(low, inv_hi, NT)

    ortho_out[...] = (0.05 * times_inverse(power[...])).astype(bf16)
    for d in range(1, 8):
        src = (me_col + d) % 8
        arrive(pperm.at[:, pl.ds(pl.multiple_of(src * 16, 16), 16)], p2s.at[d], p2r.at[src])
    served = times_inverse(pperm[...].reshape(768, 512))

    for h in range(2):
        a, b = axes[h]
        for d in (1, 3, 2):
            src = (a + d) % 4
            arrive(zo.at[h, pl.ds(pl.multiple_of(src * 128, 128), 128)], z4s.at[h, d], z4r.at[h, src])

    squares = jnp.zeros((512, 1), f32)
    for h in range(2):
        for t in range(2):
            z_hi, z_lo = split(zo[h, :, t * 512:t * 512 + 512])
            right = mm(inv_hi, z_hi) + mm(inv_hi, z_lo) + mm(inv_lo, z_hi)
            high, low = split(right)
            cols = slice(h * 1024 + t * 512, h * 1024 + t * 512 + 512)
            rt_hi[:, cols] = high
            rt_lo[:, cols] = low
            squares = squares + jnp.sum(right * right, axis=1, keepdims=True)
    flat = jnp.sum(jnp.where(ii == jj, squares, 0.0), axis=0, keepdims=True)
    csq[...] = jnp.broadcast_to(flat, (8, 512))
    for d in range(1, 8):
        to = (me_col + d) % 8
        send(csq, cfrom.at[me_col], cs.at[d], cr.at[me_col], (me_row, to))
    total = csq[...]
    for d in range(1, 8):
        src = (me_col + d) % 8
        arrive(cfrom.at[src], cs.at[d], cr.at[src])
        total = total + cfrom[src]
    scale = 1.0 / jnp.sqrt(total + 1e-06)
    scale_out[...] = scale
    coefficient = learn_rate * (ROWS / N) ** 0.5
    high, low = split(served * (-coefficient * scale[:1]))
    oph_out[...] = high
    opl_out[...] = low

    for copy in pending:
        copy.wait_send()


def finish(mom, grad, ortho, oph, opl, rt_hi, rt_lo, scale, new_mom, new_fac, served):
    r_hi, r_lo = rt_hi[...], rt_lo[...]
    new_mom[...] = mom[...] + grad[...].astype(f32) - mm(ortho[...], r_hi)
    served[...] = mm(oph[...], r_hi) + mm(oph[...], r_lo) + mm(opl[...], r_hi)
    new_fac[...] = (r_hi.astype(f32) + r_lo.astype(f32)).T * scale[:1]


def body(momentum, gradient, factor, serve_perm):
    vmem = pl.BlockSpec(memory_space=pltpu.VMEM)
    anywhere = pl.BlockSpec(memory_space=pl.ANY)
    V = pltpu.VMEM
    D = pltpu.SemaphoreType.DMA
    shape = jax.ShapeDtypeStruct
    rt_hi, rt_lo, ortho, oph, opl, scale = pl.pallas_call(
        fused,
        out_shape=(shape((512, 2048), bf16), shape((512, 2048), bf16), shape((768, 512), bf16),
                   shape((768, 512), bf16), shape((768, 512), bf16), shape((8, 512), f32)),
        in_specs=[pl.BlockSpec(memory_space=pltpu.SMEM), anywhere, anywhere, anywhere],
        out_specs=(vmem,) * 6,
        scratch_shapes=[
            V((768, 2048), f32), V((768, 2048), bf16), V((2048, 512), f32),
            V((768, 2048), bf16), V((768, 2048), bf16), V((2048, 512), bf16), V((2048, 512), bf16),
            V((768, 512), f32), V((4, 96, 512), f32), V((4, 96, 512), f32), V((4, 96, 512), f32),
            V((768, 512), f32), V((512, 768), bf16), V((512, 768), bf16),
            V((64, 512), f32), V((16, 8, 256), f32), V((512, 512), f32), V((512, 512), f32),
            V((2, 512, 1024), f32), V((2, 4, 128, 1024), f32), V((2, 128, 1024), f32),
            V((2, 4, 32, 1024), f32), V((2, 512, 1024), f32),
            V((16, 16, 512), f32), V((16, 16, 512), f32), V((6, 16, 512), f32), V((6, 128, 512), f32),
            V((8, 512), f32), V((8, 8, 512), f32),
            D((5,)), D((4,)), D((4,)), D((4,)), D((4,)), D((4,)), D((4,)), D((4,)), D((4,)),
            D((16,)), D((16,)), D((16,)), D((16,)), D((4,)), D((4,)), D((4,)), D((4,)),
            D((2, 4)), D((2, 4)), D((2, 4)), D((2, 4)), D((2, 4)), D((2, 4)), D((2, 4)), D((2, 4)),
            D((16,)), D((16,)), D((8,)), D((8,)), D((8,)), D((8,)),
        ],
        compiler_params=pltpu.CompilerParams(
            collective_id=0, has_side_effects=True, vmem_limit_bytes=60 * 1024 * 1024),
        name="factorize",
    )(serve_perm, momentum, gradient, factor)

    def tall(i):
        return (0, i)

    def whole(i):
        return (0, 0)

    return pl.pallas_call(
        finish,
        grid=(8,),
        out_shape=(shape((768, 2048), f32), shape((2048, 512), f32), shape((768, 2048), f32)),
        in_specs=[pl.BlockSpec((768, 256), tall), pl.BlockSpec((768, 256), tall),
                  pl.BlockSpec((768, 512), whole), pl.BlockSpec((768, 512), whole),
                  pl.BlockSpec((768, 512), whole),
                  pl.BlockSpec((512, 256), tall), pl.BlockSpec((512, 256), tall),
                  pl.BlockSpec((8, 512), whole)],
        out_specs=(pl.BlockSpec((768, 256), tall), pl.BlockSpec((256, 512), lambda i: (i, 0)),
                   pl.BlockSpec((768, 256), tall)),
        compiler_params=pltpu.CompilerParams(vmem_limit_bytes=60 * 1024 * 1024),
        cost_estimate=pl.CostEstimate(flops=8 * 768 * 2048 * 512, bytes_accessed=30 * 2**20, transcendentals=0),
        name="outputs",
    )(momentum, gradient, ortho, oph, opl, rt_hi, rt_lo, scale)


def solution(mesh):
    return jax.shard_map(
        body,
        mesh=mesh,
        in_specs=(P("row", "col"), P("row", "col"), P("col", None), P()),
        out_specs=(P("row", "col"), P("col", None), P("row", "col")),
        check_vma=False,
    )
```

time: 891 us -> 166 us (0.19)
  the two profiles are of different devices: /device:TPU:125 before, /device:TPU:1 now
where the time goes in v1:
time: 166 us
  Pallas kernels  165 us (99%)
    pallas_call x1, Pallas kernels, body(): pl.pallas_call(fused, out_shape=(shape((512, 2048), bf16), shape((512, 20...  149 us
    pallas_call x1, Pallas kernels, body(): pl.pallas_call(finish, grid=(8,), out_shape=(shape((768, 2048), f32), sha...  16.3 us

profile of v1, /device:TPU:1, one launch (start us, length us, event | category | flops | bytes accessed | tf_op | source)
XLA Modules:
  0.0 165.8 jit_solution(5254193400594432455)
XLA Ops:
  0.6 148.9 %factorize.1 = (bf16[512,2048]{1,0:T(8,128)(2,1)}, bf16[512,2048]{1,0:T(8,128)(2,1)}, bf16[768,512]{1,0:T(8,128)(2,1)}, bf16[768,512]{1,0:T(8,128)(2,1)}, bf16[768,512]{1,0:T(8,128)(2,1)}, /*index=5*/f32[8,512]{1,0:T(8,128)}) custom-call(s32[96]{0:T(128)} %perm_ref.1, f32[768,2048]{1,0:T(8,128)} %mom.1, bf16[768,2048]{1,0:T(8,128)(2,1)} %grad.1, ...), custom_call_target="tpu_custom_call" | custom-call | tf_op jit(solution)/shard_map/factorize/pallas_call | solution.py:397
  149.5 16.3 %outputs.1 = (f32[768,2048]{1,0:T(8,128)}, f32[2048,512]{1,0:T(8,128)}, f32[768,2048]{1,0:T(8,128)}) custom-call(f32[768,2048]{1,0:T(8,128)} %mom.1, bf16[768,2048]{1,0:T(8,128)(2,1)} %grad.1, bf16[768,512]{1,0:T(8,128)(2,1)} %get-tuple-element.9.ortho, bf16[768,512]{1,0:T(8,128)(2,1)} %get-tuple-element.10.oph, bf16[768,512]{1,0:T(8,128)(2,1)} %get-tuple-element.11.opl, ...), custom_call_target="tpu_custom_call" | custom-call | flops 6442450944 | bytes 31457280 | tf_op jit(solution)/shard_map/outputs/pallas_call | solution.py:429

commit v2 on v0

v2 whole, which is shorter than its diff:
```python
import jax
import jax.numpy as jnp
from jax import lax
from jax.experimental import pallas as pl
from jax.experimental.pallas import tpu as pltpu
from jax.sharding import PartitionSpec as P

N = 16384
ROWS = 12288
RANK = 512
learn_rate = 0.01

f32 = jnp.float32
bf16 = jnp.bfloat16
HIGHEST = lax.Precision.HIGHEST
MESH = pl.DeviceIdType.MESH
NN = (((1,), (0,)), ((), ()))
NT = (((1,), (1,)), ((), ()))


def mm(a, b, dims=NN):
    return lax.dot_general(a, b, dims, preferred_element_type=f32)


def mm_exact(a, b, dims=NN):
    return lax.dot_general(a, b, dims, precision=HIGHEST, preferred_element_type=f32)


def split(a):
    high = a.astype(bf16)
    return high, (a - high.astype(f32)).astype(bf16)


def eliminate(block):
    lane = lax.broadcasted_iota(jnp.int32, (8, 128), 1)
    sub = lax.broadcasted_iota(jnp.int32, (8, 128), 0)
    done = []
    rest = block
    for first in range(0, 128, 8):
        height = 128 - first
        cols = [jnp.broadcast_to(rest[:, first + j:first + j + 1], (height, 128)) for j in range(8)]
        inside = (lane >= first) & (lane < first + 8)
        tile = jnp.where(inside, 0.0, rest[:8])
        factors, rows = [], []
        for i in range(8):
            scale = lax.rsqrt(jnp.broadcast_to(cols[i][i:i + 1], (8, 128)))
            column = cols[i] * scale[:1]
            factors.append(column)
            for j in range(i + 1, 8):
                cols[j] = cols[j] - column * column[j:j + 1]
            row = jnp.broadcast_to(jnp.where(lane == first + i, 1.0, tile)[i:i + 1], (8, 128)) * scale
            rows.append(row)
            tile = jnp.where(sub > i, tile - column[:8] * row, jnp.where(sub == i, row, tile))
        done.append(tile)
        if height > 8:
            wide = lax.broadcasted_iota(jnp.int32, (height - 8, 128), 1)
            rest = jnp.where((wide >= first) & (wide < first + 8), 0.0, rest[8:])
            for i in range(8):
                rest = rest - factors[i][8:] * rows[i][:1]
    return jnp.concatenate(done, axis=0)


class Ring:
    def __init__(self, a, peer, ssem, rsem, pending):
        self.a, self.peer, self.ssem, self.rsem, self.pending = a, peer, ssem, rsem, pending
        self.up, self.down, self.far = (a + 1) % 4, (a + 3) % 4, (a + 2) % 4

    def send(self, i, src, dst, to):
        copy = pltpu.make_async_remote_copy(src_ref=src, dst_ref=dst, send_sem=self.ssem(i), recv_sem=self.rsem(i),
                                            device_id=self.peer(to), device_id_type=MESH)
        copy.start()
        self.pending.append(copy)

    def arrive(self, i, dst):
        pltpu.make_async_remote_copy(src_ref=dst, dst_ref=dst, send_sem=self.ssem(i), recv_sem=self.rsem(i),
                                     device_id=self.peer(self.up), device_id_type=MESH).wait_recv()


class Reduce(Ring):
    def bind(self, chunk, relay, land):
        self.chunk, self.relay_ref, self.land = chunk, relay, land
        return self

    def start_far(self):
        self.send(0, self.chunk(self.far, 0), self.relay_ref(0), self.up)
        self.send(1, self.chunk(self.far, 1), self.relay_ref(1), self.down)

    def start_near(self):
        self.send(2, self.chunk(self.up, 1), self.land(0, 1), self.up)
        self.send(3, self.chunk(self.down, 0), self.land(1, 0), self.down)

    def start(self):
        self.start_far()
        self.start_near()

    def relay(self):
        for w, to in ((0, self.up), (1, self.down)):
            ref = self.relay_ref(w)
            self.arrive(w, ref)
            ref[...] = ref[...] + self.chunk(to, w)[...]
            self.send(4 + w, ref, self.land(w, w), to)

    def finish(self, h):
        self.arrive(2 + 1 - h, self.land(1 - h, h))
        self.arrive(4 + h, self.land(h, h))
        return self.chunk(self.a, h)[...] + self.land(0, h)[...] + self.land(1, h)[...]


class Gather(Ring):
    def bind(self, chunk):
        self.chunk = chunk
        return self

    def post(self, i, c, h, to):
        self.send(i, self.chunk(c, h), self.chunk(c, h), to)

    def start(self):
        self.post(0, self.a, 0, self.up)
        self.post(1, self.a, 1, self.down)
        self.post(2, self.a, 1, self.up)
        self.post(3, self.a, 0, self.down)

    def relay(self):
        self.arrive(0, self.chunk(self.down, 0))
        self.post(4, self.down, 0, self.up)
        self.arrive(1, self.chunk(self.up, 1))
        self.post(5, self.up, 1, self.down)

    def finish(self):
        self.arrive(2, self.chunk(self.down, 1))
        self.arrive(3, self.chunk(self.up, 0))
        self.arrive(4, self.chunk(self.far, 0))
        self.arrive(5, self.chunk(self.far, 1))


class DirectReduce(Ring):
    def bind(self, chunk, land):
        self.chunk, self.land = chunk, land
        return self

    def start(self):
        for i, to in enumerate((self.far, self.up, self.down)):
            self.send(i, self.chunk(to), self.land(i), to)

    def finish(self):
        total = self.chunk(self.a)[...]
        for i in (1, 2, 0):
            self.arrive(i, self.land(i))
            total = total + self.land(i)[...]
        return total


class DirectGather(Ring):
    def bind(self, chunk):
        self.chunk = chunk
        return self

    def start(self):
        for i, to in enumerate((self.far, self.up, self.down)):
            self.send(i, self.chunk(self.a), self.chunk(self.a), to)

    def finish(self):
        for i, src in ((1, self.down), (2, self.up), (0, self.far)):
            self.arrive(i, self.chunk(src))


def fused(perm_ref, mom_hbm, grad_hbm, fac_hbm,
          rt_hi_out, rt_lo_out, ortho_out, oph_out, opl_out, scale_out,
          mom, grad, fac, buf_hi, buf_lo, fac_hi, fac_lo, part, from_core, to_y, rel_y, land_y,
          power, pt_hi, pt_lo, gpart, gfrom, gram, work, zt, rel1, land1, zsum1, land2, zo,
          psend, pfrom, ppiece, pperm, csq, cfrom, rt_hi, rt_lo, ortho, oph, opl, scale,
          lsem, a1s, a1r, ys, yr, ms, mr, g1s, g1r, g2s, g2r, g3s, g3r, g4s, g4r,
          zs, zr, p1s, p1r, p2s, p2r, cs, cr, osem):
    me_row = lax.axis_index("row")
    me_col = lax.axis_index("col")
    x, z = me_row // 4, me_row % 4
    y, core = me_col // 2, me_col % 2
    mate = (me_row, y * 2 + 1 - core)
    pending = []

    def send(src, dst, ssem, rsem, dev):
        copy = pltpu.make_async_remote_copy(src_ref=src, dst_ref=dst, send_sem=ssem, recv_sem=rsem,
                                            device_id=dev, device_id_type=MESH)
        copy.start()
        pending.append(copy)

    def arrive(dst, ssem, rsem):
        pltpu.make_async_remote_copy(src_ref=dst, dst_ref=dst, send_sem=ssem, recv_sem=rsem,
                                     device_id=mate, device_id_type=MESH).wait_recv()

    def ds(start, size):
        return pl.ds(pl.multiple_of(start, size), size)

    other = pl.multiple_of((1 - core) * 384, 384)
    mine = pl.multiple_of(core * 384, 384)

    def load(h, k):
        rows = pl.ds(other if h == 0 else mine, 384)
        cols = ds(k * 256, 256)
        copies = [pltpu.make_async_copy(mom_hbm.at[rows, cols], mom.at[rows, cols], lsem.at[h, 0, k]),
                  pltpu.make_async_copy(grad_hbm.at[rows, cols], grad.at[rows, cols], lsem.at[h, 1, k])]
        if h == 0:
            copies.append(pltpu.make_async_copy(fac_hbm.at[cols], fac.at[cols], lsem.at[h, 2, k]))
        return copies

    for h in range(2):
        for k in range(8):
            for copy in load(h, k):
                copy.start()

    barrier = pltpu.get_barrier_semaphore()
    for d in range(1, 16):
        pl.semaphore_signal(barrier, inc=1, device_id=((me_row + d) % 16, me_col), device_id_type=MESH)
    for d in range(1, 8):
        pl.semaphore_signal(barrier, inc=1, device_id=(me_row, (me_col + d) % 8), device_id_type=MESH)

    def cols_of(n):
        return slice(n * 256, n * 256 + 256)

    def prepare(h, k):
        for copy in load(h, k):
            copy.wait()
        rows = pl.ds(other if h == 0 else mine, 384)
        cols = ds(k * 256, 256)
        high, low = split(mom[rows, cols] + grad[rows, cols].astype(f32))
        buf_hi[rows, cols] = high
        buf_lo[rows, cols] = low
        if h == 0:
            high, low = split(fac[cols, :])
            fac_hi[cols, :] = high
            fac_lo[cols, :] = low

    def power_block(h, n, k):
        rows = pl.ds(other if h == 0 else mine, 384)
        cols = ds(k * 256, 256)
        c = cols_of(n)
        part[rows, c] = part[rows, c] + (mm(buf_hi[rows, cols], fac_hi[cols, c])
                                         + mm(buf_hi[rows, cols], fac_lo[cols, c])
                                         + mm(buf_lo[rows, cols], fac_hi[cols, c]))

    def power_part(h, n):
        part[pl.ds(other if h == 0 else mine, 384), cols_of(n)] = jnp.zeros((384, 256), f32)
        if n == 0:
            prepare(h, 0)

        @pl.loop(0, 7)
        def _(k):
            if n == 0:
                prepare(h, k + 1)
            power_block(h, n, k)

        power_block(h, n, 7)

    order = (2, 1, 3, 0)

    def core_start(n):
        for d in order:
            to = (y + d) % 4
            send(part.at[ds(other + to * 96, 96), cols_of(n)], from_core.at[n, to],
                 a1s.at[n, d], a1r.at[n, d], mate)

    def core_add(n, d):
        to = (y + d) % 4
        arrive(from_core.at[n, to], a1s.at[n, d], a1r.at[n, d])
        to_y[n, to] = part[ds(mine + to * 96, 96), cols_of(n)] + from_core[n, to]

    def y_peer(to):
        return (me_row, to * 2 + core)

    def half(c, h, size):
        return ds(c * size * 2 + h * size, size)

    def spot(base, c, h):
        return pl.ds(pl.multiple_of(base + c * 96 + h * 48, 48), 48)

    y_sum = [Reduce(y, y_peer, lambda i, n=n: ys.at[0, n, i], lambda i, n=n: yr.at[0, n, i], pending).bind(
        lambda c, h, n=n: to_y.at[n, c, pl.ds(h * 48, 48)],
        lambda w, n=n: rel_y.at[n, w],
        lambda w, h, n=n: land_y.at[n, w, pl.ds(h * 48, 48)]) for n in range(2)]
    y_all = [Gather(y, y_peer, lambda i, n=n: ys.at[1, n, i], lambda i, n=n: yr.at[1, n, i], pending).bind(
        lambda c, h, n=n: power.at[spot(mine, c, h), cols_of(n)]) for n in range(2)]

    def y_start(n):
        core_add(n, 2)
        y_sum[n].start_far()
        core_add(n, 1)
        core_add(n, 3)
        y_sum[n].start_near()

    def to_mate(n, d, h):
        piece = power.at[spot(mine, (y + d) % 4, h), cols_of(n)]
        send(piece, piece, ms.at[n, d, h], mr.at[n, d, h], mate)

    def y_second(n):
        core_add(n, 0)
        for h in range(2):
            power[spot(mine, y, h), cols_of(n)] = y_sum[n].finish(h)
        y_all[n].start()
        for h in range(2):
            to_mate(n, 0, h)

    def y_third(n):
        y_all[n].relay()
        to_mate(n, 3, 0)
        to_mate(n, 1, 1)

    def y_end(n):
        y_all[n].finish()
        for d, h in ((3, 1), (1, 0), (2, 0), (2, 1)):
            to_mate(n, d, h)
        for d, h in ((0, 0), (0, 1), (3, 0), (1, 1), (3, 1), (1, 0), (2, 0), (2, 1)):
            piece = power.at[spot(other, (y + d) % 4, h), cols_of(n)]
            arrive(piece, ms.at[n, d, h], mr.at[n, d, h])
        for j in range(6):
            high, low = split(power[j * 128:j * 128 + 128, cols_of(n)].T)
            pt_hi[cols_of(n), j * 128:j * 128 + 128] = high
            pt_lo[cols_of(n), j * 128:j * 128 + 128] = low

    axes = ((x, z), (z, x))

    def z_peer(h, level):
        along_x = (h == 0) == (level == 0)
        return lambda to: (to * 4 + z, me_col) if along_x else (x * 4 + to, me_col)

    def z_sems(stage, n, h):
        return (lambda i: zs.at[stage, n, h, i]), (lambda i: zr.at[stage, n, h, i])

    pairs = [(n, h) for n in range(2) for h in range(2)]
    z_one, z_two, z_three, z_four = {}, {}, {}, {}
    for n, h in pairs:
        a, b = axes[h]
        z_one[n, h] = Reduce(a, z_peer(h, 0), *z_sems(0, n, h), pending).bind(
            lambda c, t, n=n, h=h: zt.at[n, h, half(c, t, 32)],
            lambda w, n=n, h=h: rel1.at[n, h, w],
            lambda w, t, n=n, h=h: land1.at[n, h, w, pl.ds(t * 32, 32)])
        z_two[n, h] = DirectReduce(b, z_peer(h, 1), *z_sems(1, n, h), pending).bind(
            lambda c, n=n, h=h: zsum1.at[n, h, ds(c * 16, 16)],
            lambda i, n=n, h=h: land2.at[n, h, i])
        z_three[n, h] = DirectGather(b, z_peer(h, 1), *z_sems(2, n, h), pending).bind(
            lambda c, n=n, h=h, a=a: zo.at[n, h, ds(a * 64 + c * 16, 16)])
        z_four[n, h] = Gather(a, z_peer(h, 0), *z_sems(3, n, h), pending).bind(
            lambda c, t, n=n, h=h: zo.at[n, h, half(c, t, 32)])

    def z_compute(n, h):
        @pl.loop(0, 2)
        def _(t):
            cols = ds(h * 1024 + t * 512, 512)
            zt[n, h, :, ds(t * 512, 512)] = (
                mm(pt_hi[cols_of(n), :], buf_hi[:, cols]) + mm(pt_hi[cols_of(n), :], buf_lo[:, cols])
                + mm(pt_lo[cols_of(n), :], buf_hi[:, cols]))

    def both(table, n):
        for h in range(2):
            table[n, h].relay()

    def starts(table, n):
        for h in range(2):
            table[n, h].start()

    def z_second(n):
        for h in range(2):
            for t in range(2):
                zsum1[n, h, t * 32:t * 32 + 32, :] = z_one[n, h].finish(t)

    def z_third(n):
        for h in range(2):
            a, b = axes[h]
            zo[n, h, ds(a * 64 + b * 16, 16), :] = z_two[n, h].finish()
            z_three[n, h].start()

    def z_fourth(n):
        for h in range(2):
            z_three[n, h].finish()
            z_four[n, h].start()

    def z_end(n):
        for h in range(2):
            z_four[n, h].finish()

    strip = ds(me_col * 64, 64)

    def unit(r, base=0):
        return (ds(base + (r // 2) * 8, 8), ds((r % 2) * 256, 256))

    def gram_start():
        p_hi, p_lo = pt_hi[strip, :], pt_lo[strip, :]
        gpart[...] = (mm(p_hi, pt_hi[...], NT) + mm(p_hi, pt_lo[...], NT)
                      + mm(p_lo, pt_hi[...], NT) + mm(p_lo, pt_lo[...], NT))
        for d in range(1, 16):
            to = (me_row + d) % 16
            send(gpart.at[unit(to)], gfrom.at[me_row], g1s.at[d], g1r.at[me_row], (to, me_col))

    def gram_second():
        total = gpart[unit(me_row)]
        for d in range(1, 16):
            src = (me_row + d) % 16
            arrive(gfrom.at[src], g1s.at[d], g1r.at[src])
            total = total + gfrom[src]
        gram[unit(me_row, me_col * 64)] = total
        for d in range(1, 16):
            to = (me_row + d) % 16
            piece = gram.at[unit(me_row, me_col * 64)]
            send(piece, piece, g2s.at[d], g2r.at[me_row], (to, me_col))

    def strip_half(c, h, k):
        return gram.at[ds((c * 2 + k) * 64 + h * 32, 32)]

    strips = Gather(y, y_peer, lambda i: g3s.at[i], lambda i: g3r.at[i], pending).bind(
        lambda c, h: strip_half(c, h, core))

    def strip_to_mate(d, h):
        piece = strip_half((y + d) % 4, h, core)
        send(piece, piece, g4s.at[d, h], g4r.at[d, h], mate)

    def gram_third():
        for d in range(1, 16):
            src = (me_row + d) % 16
            arrive(gram.at[unit(src, me_col * 64)], g2s.at[d], g2r.at[src])
        strips.start()
        strip_to_mate(0, 0)
        strip_to_mate(0, 1)

    def gram_fourth():
        strips.relay()
        strip_to_mate(3, 0)
        strip_to_mate(1, 1)

    def gram_end():
        strips.finish()
        for d, h in ((3, 1), (1, 0), (2, 0), (2, 1)):
            strip_to_mate(d, h)
        for d, h in ((0, 0), (0, 1), (3, 0), (1, 1), (3, 1), (1, 0), (2, 0), (2, 1)):
            arrive(strip_half((y + d) % 4, h, 1 - core), g4s.at[d, h], g4r.at[d, h])
        work[...] = gram[...]

    def pick(dest):
        local = jnp.int32(0)
        for t in range(6):
            b = perm_ref[dest * 6 + t] - me_row * 6
            local = local + jnp.where((b >= 0) & (b < 6), b, 0)
        share = power[ds(me_col * 16, 16), :]
        for l in range(1, 6):
            share = jnp.where(local == l, power[ds(l * 128 + me_col * 16, 16), :], share)
        return share

    def perm_start():
        for d in range(1, 16):
            to = (me_row + d) % 16
            psend[d] = pick(to)
            send(psend.at[d], pfrom.at[me_row], p1s.at[d], p1r.at[me_row], (to, me_col))
        pfrom[me_row] = pick(me_row)

    def perm_second():
        for d in range(1, 16):
            src = (me_row + d) % 16
            arrive(pfrom.at[src], p1s.at[d], p1r.at[src])
        for t in range(6):
            first = perm_ref[me_row * 6 + t]
            share = pfrom[0]
            for r in range(1, 16):
                share = jnp.where(first >= r * 6, pfrom[r], share)
            ppiece[t] = share
        mine_rows = ds(me_col * 16, 16)
        pperm[:, mine_rows, :] = ppiece[...]
        for d in range(1, 8):
            to = (me_col + d) % 8
            send(ppiece, pperm.at[:, mine_rows], p2s.at[d], p2r.at[me_col], (me_row, to))

    li = lax.broadcasted_iota(jnp.int32, (128, 128), 0)
    lj = lax.broadcasted_iota(jnp.int32, (128, 128), 1)

    def factor_block(k):
        s = slice(128 * k, 128 * k + 128)
        inv = jnp.where(li >= lj, eliminate(work[s, s]), 0.0)
        work[s, s] = jnp.where(li == lj, 1.0, 0.0)
        row = mm_exact(inv, work[s, :])
        work[s, :] = row
        if k < 3:
            r = slice(128 * k + 128, 512)
            low = mm_exact(work[r, s], inv, NT)
            work[r, s] = jnp.zeros((512 - 128 * k - 128, 128), f32)
            work[r, :] = work[r, :] - mm_exact(low, row)

    power_part(0, 0)
    pl.semaphore_wait(barrier, 22)
    core_start(0)
    power_part(1, 0)
    power_part(0, 1)
    core_start(1)
    y_start(0)
    power_part(1, 1)
    y_sum[0].relay()
    y_start(1)
    y_second(0)
    y_sum[1].relay()
    y_third(0)
    y_second(1)
    y_end(0)
    y_third(1)
    for h in range(2):
        z_compute(0, h)
        z_one[0, h].start()
    y_end(1)
    gram_start()
    both(z_one, 0)
    z_compute(1, 0)
    z_compute(1, 1)
    gram_second()
    z_second(0)
    starts(z_two, 0)
    gram_third()
    perm_start()
    starts(z_one, 1)
    gram_fourth()
    z_third(0)
    both(z_one, 1)
    gram_end()
    z_fourth(0)
    factor_block(0)
    z_second(1)
    starts(z_two, 1)
    perm_second()
    both(z_four, 0)
    factor_block(1)
    z_third(1)
    factor_block(2)
    z_fourth(1)
    factor_block(3)
    both(z_four, 1)

    ii = lax.broadcasted_iota(jnp.int32, (512, 512), 0)
    jj = lax.broadcasted_iota(jnp.int32, (512, 512), 1)
    inv_hi, inv_lo = split(jnp.where(ii >= jj, work[...], 0.0))

    def times_inverse(block):
        high, low = split(block)
        parts = []
        for top, k in ((0, 256), (256, 512)):
            h, l = high[:, :k], low[:, :k]
            i_hi, i_lo = inv_hi[top:top + 256, :k], inv_lo[top:top + 256, :k]
            parts.append(mm(h, i_hi, NT) + mm(h, i_lo, NT) + mm(l, i_hi, NT))
        return jnp.concatenate(parts, axis=1)

    copies = []

    def put(src, dst):
        copy = pltpu.make_async_copy(src, dst, osem.at[len(copies)])
        copy.start()
        copies.append(copy)

    z_end(0)
    z_end(1)

    squares = jnp.zeros((512, 1), f32)
    for h in range(2):
        for t in range(2):
            c = slice(t * 512, t * 512 + 512)
            z_hi, z_lo = split(zo[:, h, :, c].reshape(512, 512))
            parts = []
            for top, k in ((0, 256), (256, 512)):
                i_hi, i_lo = inv_hi[top:top + 256, :k], inv_lo[top:top + 256, :k]
                parts.append(mm(i_hi, z_hi[:k]) + mm(i_hi, z_lo[:k]) + mm(i_lo, z_hi[:k]))
            right = jnp.concatenate(parts, axis=0)
            high, low = split(right)
            cols = slice(h * 1024 + t * 512, h * 1024 + t * 512 + 512)
            rt_hi[:, cols] = high
            rt_lo[:, cols] = low
            put(rt_hi.at[:, cols], rt_hi_out.at[:, cols])
            put(rt_lo.at[:, cols], rt_lo_out.at[:, cols])
            squares = squares + jnp.sum(right * right, axis=1, keepdims=True)
    flat = jnp.sum(jnp.where(ii == jj, squares, 0.0), axis=0, keepdims=True)
    csq[...] = jnp.broadcast_to(flat, (8, 512))
    for d in range(1, 8):
        to = (me_col + d) % 8
        send(csq, cfrom.at[me_col], cs.at[d], cr.at[me_col], (me_row, to))

    ortho[...] = (0.05 * times_inverse(power[...])).astype(bf16)
    put(ortho, ortho_out)
    for d in range(1, 8):
        src = (me_col + d) % 8
        arrive(pperm.at[:, ds(src * 16, 16)], p2s.at[d], p2r.at[src])
    served = times_inverse(pperm[...].reshape(768, 512))

    total = csq[...]
    for d in range(1, 8):
        src = (me_col + d) % 8
        arrive(cfrom.at[src], cs.at[d], cr.at[src])
        total = total + cfrom[src]
    root = 1.0 / jnp.sqrt(total + 1e-06)
    scale[...] = root
    put(scale, scale_out)
    coefficient = learn_rate * (ROWS / N) ** 0.5
    high, low = split(served * (-coefficient * root[:1]))
    oph[...] = high
    opl[...] = low
    put(oph, oph_out)
    put(opl, opl_out)
    for copy in copies:
        copy.wait()

    for copy in pending:
        copy.wait_send()


def finish(mom, grad, ortho, oph, opl, rt_hi, rt_lo, scale, new_mom, new_fac, served):
    r_hi, r_lo = rt_hi[...], rt_lo[...]
    new_mom[...] = mom[...] + grad[...].astype(f32) - mm(ortho[...], r_hi)
    served[...] = mm(oph[...], r_hi) + mm(oph[...], r_lo) + mm(opl[...], r_hi)
    new_fac[...] = (r_hi.astype(f32) + r_lo.astype(f32)).T * scale[:1]


def body(momentum, gradient, factor, serve_perm):
    anywhere = pl.BlockSpec(memory_space=pl.ANY)
    V = pltpu.VMEM
    D = pltpu.SemaphoreType.DMA
    shape = jax.ShapeDtypeStruct
    rt_hi, rt_lo, ortho, oph, opl, scale = pl.pallas_call(
        fused,
        out_shape=(shape((512, 2048), bf16), shape((512, 2048), bf16), shape((768, 512), bf16),
                   shape((768, 512), bf16), shape((768, 512), bf16), shape((8, 512), f32)),
        in_specs=[pl.BlockSpec(memory_space=pltpu.SMEM), anywhere, anywhere, anywhere],
        out_specs=(anywhere,) * 6,
        scratch_shapes=[
            V((768, 2048), f32), V((768, 2048), bf16), V((2048, 512), f32),
            V((768, 2048), bf16), V((768, 2048), bf16), V((2048, 512), bf16), V((2048, 512), bf16),
            V((768, 512), f32), V((2, 4, 96, 256), f32), V((2, 4, 96, 256), f32),
            V((2, 2, 48, 256), f32), V((2, 2, 96, 256), f32),
            V((768, 512), f32), V((512, 768), bf16), V((512, 768), bf16),
            V((64, 512), f32), V((16, 8, 256), f32), V((512, 512), f32), V((512, 512), f32),
            V((2, 2, 256, 1024), f32), V((2, 2, 2, 32, 1024), f32), V((2, 2, 2, 64, 1024), f32),
            V((2, 2, 64, 1024), f32), V((2, 2, 3, 16, 1024), f32),
            V((2, 2, 256, 1024), f32),
            V((16, 16, 512), f32), V((16, 16, 512), f32), V((6, 16, 512), f32), V((6, 128, 512), f32),
            V((8, 512), f32), V((8, 8, 512), f32), V((512, 2048), bf16), V((512, 2048), bf16),
            V((768, 512), bf16), V((768, 512), bf16), V((768, 512), bf16), V((8, 512), f32),
            D((2, 3, 8)), D((2, 4)), D((2, 4)), D((2, 2, 6)), D((2, 2, 6)), D((2, 4, 2)), D((2, 4, 2)),
            D((16,)), D((16,)), D((16,)), D((16,)), D((6,)), D((6,)), D((4, 2)), D((4, 2)),
            D((4, 2, 2, 6)), D((4, 2, 2, 6)),
            D((16,)), D((16,)), D((8,)), D((8,)), D((8,)), D((8,)), D((12,)),
        ],
        compiler_params=pltpu.CompilerParams(
            collective_id=0, has_side_effects=True, vmem_limit_bytes=60 * 1024 * 1024),
        name="factorize",
    )(serve_perm, momentum, gradient, factor)

    def tall(i):
        return (0, i)

    def whole(i):
        return (0, 0)

    return pl.pallas_call(
        finish,
        grid=(4,),
        out_shape=(shape((768, 2048), f32), shape((2048, 512), f32), shape((768, 2048), f32)),
        in_specs=[pl.BlockSpec((768, 512), tall), pl.BlockSpec((768, 512), tall),
                  pl.BlockSpec((768, 512), whole), pl.BlockSpec((768, 512), whole),
                  pl.BlockSpec((768, 512), whole),
                  pl.BlockSpec((512, 512), tall), pl.BlockSpec((512, 512), tall),
                  pl.BlockSpec((8, 512), whole)],
        out_specs=(pl.BlockSpec((768, 512), tall), pl.BlockSpec((512, 512), lambda i: (i, 0)),
                   pl.BlockSpec((768, 512), tall)),
        compiler_params=pltpu.CompilerParams(vmem_limit_bytes=60 * 1024 * 1024),
        cost_estimate=pl.CostEstimate(flops=8 * 768 * 2048 * 512, bytes_accessed=30 * 2**20, transcendentals=0),
        name="outputs",
    )(momentum, gradient, ortho, oph, opl, rt_hi, rt_lo, scale)


def solution(mesh):
    return jax.shard_map(
        body,
        mesh=mesh,
        in_specs=(P("row", "col"), P("row", "col"), P("col", None), P()),
        out_specs=(P("row", "col"), P("col", None), P("row", "col")),
        check_vma=False,
    )
```

time: 891 us -> 138 us (0.15)
  the two profiles are of different devices: /device:TPU:125 before, /device:TPU:1 now
where the time goes in v2:
time: 138 us
  Pallas kernels  137 us (99%)
    pallas_call x1, Pallas kernels, body(): pl.pallas_call(fused, out_shape=(shape((512, 2048), bf16), shape((512, 20...  123 us
    pallas_call x1, Pallas kernels, body(): pl.pallas_call(finish, grid=(4,), out_shape=(shape((768, 2048), f32), sha...  14.1 us

profile of v2, /device:TPU:1, one launch (start us, length us, event | category | flops | bytes accessed | tf_op | source)
XLA Modules:
  0.0 137.8 jit_solution(3922717025284109379)
XLA Ops:
  0.6 123.1 %factorize.1 = (bf16[512,2048]{1,0:T(8,128)(2,1)}, bf16[512,2048]{1,0:T(8,128)(2,1)}, bf16[768,512]{1,0:T(8,128)(2,1)}, bf16[768,512]{1,0:T(8,128)(2,1)}, bf16[768,512]{1,0:T(8,128)(2,1)}, /*index=5*/f32[8,512]{1,0:T(8,128)}) custom-call(s32[96]{0:T(128)} %perm_ref.1, f32[768,2048]{1,0:T(8,128)} %mom.1, bf16[768,2048]{1,0:T(8,128)(2,1)} %grad.1, ...), custom_call_target="tpu_custom_call" | custom-call | tf_op jit(solution)/shard_map/factorize/pallas_call | solution.py:617
  123.7 14.1 %outputs.1 = (f32[768,2048]{1,0:T(8,128)}, f32[2048,512]{1,0:T(8,128)}, f32[768,2048]{1,0:T(8,128)}) custom-call(f32[768,2048]{1,0:T(8,128)} %mom.1, bf16[768,2048]{1,0:T(8,128)(2,1)} %grad.1, bf16[768,512]{1,0:T(8,128)(2,1)} %get-tuple-element.9.ortho, bf16[768,512]{1,0:T(8,128)(2,1)} %get-tuple-element.10.oph, bf16[768,512]{1,0:T(8,128)(2,1)} %get-tuple-element.11.opl, ...), custom_call_target="tpu_custom_call" | custom-call | flops 6442450944 | bytes 31457280 | tf_op jit(solution)/shard_map/outputs/pallas_call | solution.py:652

commit v3 on v2

--- a/solution.py
+++ b/solution.py
@@ -31,12 +31,14 @@
     return high, (a - high.astype(f32)).astype(bf16)
 
 
-def eliminate(block):
+def eliminate(block, midway):
     lane = lax.broadcasted_iota(jnp.int32, (8, 128), 1)
     sub = lax.broadcasted_iota(jnp.int32, (8, 128), 0)
     done = []
     rest = block
     for first in range(0, 128, 8):
+        if first == 40:
+            midway()
         height = 128 - first
         cols = [jnp.broadcast_to(rest[:, first + j:first + j + 1], (height, 128)) for j in range(8)]
         inside = (lane >= first) & (lane < first + 8)
@@ -126,11 +128,10 @@
         self.arrive(1, self.chunk(self.up, 1))
         self.post(5, self.up, 1, self.down)
 
-    def finish(self):
-        self.arrive(2, self.chunk(self.down, 1))
-        self.arrive(3, self.chunk(self.up, 0))
-        self.arrive(4, self.chunk(self.far, 0))
-        self.arrive(5, self.chunk(self.far, 1))
+    def finish(self, then=lambda d, h: None):
+        for i, d, h in ((2, 3, 1), (3, 1, 0), (4, 2, 0), (5, 2, 1)):
+            self.arrive(i, self.chunk((self.a + d) % 4, h))
+            then(d, h)
 
 
 class DirectReduce(Ring):
@@ -184,6 +185,11 @@
         copy.start()
         pending.append(copy)
 
+    def flush():
+        for copy in pending:
+            copy.wait_send()
+        pending.clear()
+
     def arrive(dst, ssem, rsem):
         pltpu.make_async_remote_copy(src_ref=dst, dst_ref=dst, send_sem=ssem, recv_sem=rsem,
                                      device_id=mate, device_id_type=MESH).wait_recv()
@@ -305,9 +311,7 @@
         to_mate(n, 1, 1)
 
     def y_end(n):
-        y_all[n].finish()
-        for d, h in ((3, 1), (1, 0), (2, 0), (2, 1)):
-            to_mate(n, d, h)
+        y_all[n].finish(lambda d, h: to_mate(n, d, h))
         for d, h in ((0, 0), (0, 1), (3, 0), (1, 1), (3, 1), (1, 0), (2, 0), (2, 1)):
             piece = power.at[spot(other, (y + d) % 4, h), cols_of(n)]
             arrive(piece, ms.at[n, d, h], mr.at[n, d, h])
@@ -426,9 +430,7 @@
         strip_to_mate(1, 1)
 
     def gram_end():
-        strips.finish()
-        for d, h in ((3, 1), (1, 0), (2, 0), (2, 1)):
-            strip_to_mate(d, h)
+        strips.finish(strip_to_mate)
         for d, h in ((0, 0), (0, 1), (3, 0), (1, 1), (3, 1), (1, 0), (2, 0), (2, 1)):
             arrive(strip_half((y + d) % 4, h, 1 - core), g4s.at[d, h], g4r.at[d, h])
         work[...] = gram[...]
@@ -469,9 +471,9 @@
     li = lax.broadcasted_iota(jnp.int32, (128, 128), 0)
     lj = lax.broadcasted_iota(jnp.int32, (128, 128), 1)
 
-    def factor_block(k):
+    def factor_block(k, midway=lambda: None):
         s = slice(128 * k, 128 * k + 128)
-        inv = jnp.where(li >= lj, eliminate(work[s, s]), 0.0)
+        inv = jnp.where(li >= lj, eliminate(work[s, s], midway), 0.0)
         work[s, s] = jnp.where(li == lj, 1.0, 0.0)
         row = mm_exact(inv, work[s, :])
         work[s, :] = row
@@ -506,27 +508,25 @@
     z_compute(1, 0)
     z_compute(1, 1)
     gram_second()
+    starts(z_one, 1)
     z_second(0)
     starts(z_two, 0)
+    perm_start()
     gram_third()
-    perm_start()
-    starts(z_one, 1)
+    both(z_one, 1)
     gram_fourth()
-    z_third(0)
-    both(z_one, 1)
-    gram_end()
-    z_fourth(0)
-    factor_block(0)
     z_second(1)
     starts(z_two, 1)
+    gram_end()
+    z_third(0)
     perm_second()
+    factor_block(0, lambda: z_third(1))
+    z_fourth(0)
+    factor_block(1, lambda: z_fourth(1))
     both(z_four, 0)
-    factor_block(1)
-    z_third(1)
-    factor_block(2)
-    z_fourth(1)
+    factor_block(2, lambda: both(z_four, 1))
+    flush()
     factor_block(3)
-    both(z_four, 1)
 
     ii = lax.broadcasted_iota(jnp.int32, (512, 512), 0)
     jj = lax.broadcasted_iota(jnp.int32, (512, 512), 1)
@@ -651,15 +651,15 @@
 
     return pl.pallas_call(
         finish,
-        grid=(4,),
+        grid=(2,),
         out_shape=(shape((768, 2048), f32), shape((2048, 512), f32), shape((768, 2048), f32)),
-        in_specs=[pl.BlockSpec((768, 512), tall), pl.BlockSpec((768, 512), tall),
+        in_specs=[pl.BlockSpec((768, 1024), tall), pl.BlockSpec((768, 1024), tall),
                   pl.BlockSpec((768, 512), whole), pl.BlockSpec((768, 512), whole),
                   pl.BlockSpec((768, 512), whole),
-                  pl.BlockSpec((512, 512), tall), pl.BlockSpec((512, 512), tall),
+                  pl.BlockSpec((512, 1024), tall), pl.BlockSpec((512, 1024), tall),
                   pl.BlockSpec((8, 512), whole)],
-        out_specs=(pl.BlockSpec((768, 512), tall), pl.BlockSpec((512, 512), lambda i: (i, 0)),
-                   pl.BlockSpec((768, 512), tall)),
+        out_specs=(pl.BlockSpec((768, 1024), tall), pl.BlockSpec((1024, 512), lambda i: (i, 0)),
+                   pl.BlockSpec((768, 1024), tall)),
         compiler_params=pltpu.CompilerParams(vmem_limit_bytes=60 * 1024 * 1024),
         cost_estimate=pl.CostEstimate(flops=8 * 768 * 2048 * 512, bytes_accessed=30 * 2**20, transcendentals=0),
         name="outputs",

time: 138 us -> 131 us (0.949)
  Pallas kernels: 137 us -> 131 us
    pallas_call x1, Pallas kernels: 123 us -> 117 us  [body(): pl.pallas_call(fused, out_shape=(shape((512, 2048), bf16), shape((512, 20...]
where the time goes in v3:
time: 131 us
  Pallas kernels  131 us (100%)
    pallas_call x1, Pallas kernels, body(): pl.pallas_call(fused, out_shape=(shape((512, 2048), bf16), shape((512, 20...  117 us
    pallas_call x1, Pallas kernels, body(): pl.pallas_call(finish, grid=(2,), out_shape=(shape((768, 2048), f32), sha...  13.8 us

profile of v3, /device:TPU:1, one launch (start us, length us, event | category | flops | bytes accessed | tf_op | source)
XLA Modules:
  0.0 131.3 jit_solution(8657106956625166408)
XLA Ops:
  0.6 116.9 %factorize.1 = (bf16[512,2048]{1,0:T(8,128)(2,1)}, bf16[512,2048]{1,0:T(8,128)(2,1)}, bf16[768,512]{1,0:T(8,128)(2,1)}, bf16[768,512]{1,0:T(8,128)(2,1)}, bf16[768,512]{1,0:T(8,128)(2,1)}, /*index=5*/f32[8,512]{1,0:T(8,128)}) custom-call(s32[96]{0:T(128)} %perm_ref.1, f32[768,2048]{1,0:T(8,128)} %mom.1, bf16[768,2048]{1,0:T(8,128)(2,1)} %grad.1, ...), custom_call_target="tpu_custom_call" | custom-call | tf_op jit(solution)/shard_map/factorize/pallas_call | solution.py:617
  117.5 13.8 %outputs.1 = (f32[768,2048]{1,0:T(8,128)}, f32[2048,512]{1,0:T(8,128)}, f32[768,2048]{1,0:T(8,128)}) custom-call(f32[768,2048]{1,0:T(8,128)} %mom.1, bf16[768,2048]{1,0:T(8,128)(2,1)} %grad.1, bf16[768,512]{1,0:T(8,128)(2,1)} %get-tuple-element.9.ortho, bf16[768,512]{1,0:T(8,128)(2,1)} %get-tuple-element.10.oph, bf16[768,512]{1,0:T(8,128)(2,1)} %get-tuple-element.11.opl, ...), custom_call_target="tpu_custom_call" | custom-call | flops 6442450944 | bytes 31457280 | tf_op jit(solution)/shard_map/outputs/pallas_call | solution.py:652

commit v4 on v3

--- a/solution.py
+++ b/solution.py
@@ -185,10 +185,10 @@
         copy.start()
         pending.append(copy)
 
-    def flush():
-        for copy in pending:
+    def flush(count):
+        for copy in pending[:count]:
             copy.wait_send()
-        pending.clear()
+        del pending[:count]
 
     def arrive(dst, ssem, rsem):
         pltpu.make_async_remote_copy(src_ref=dst, dst_ref=dst, send_sem=ssem, recv_sem=rsem,
@@ -506,9 +506,10 @@
     gram_start()
     both(z_one, 0)
     z_compute(1, 0)
+    z_one[1, 0].start()
     z_compute(1, 1)
+    z_one[1, 1].start()
     gram_second()
-    starts(z_one, 1)
     z_second(0)
     starts(z_two, 0)
     perm_start()
@@ -518,6 +519,7 @@
     z_second(1)
     starts(z_two, 1)
     gram_end()
+    early = len(pending)
     z_third(0)
     perm_second()
     factor_block(0, lambda: z_third(1))
@@ -525,7 +527,7 @@
     factor_block(1, lambda: z_fourth(1))
     both(z_four, 0)
     factor_block(2, lambda: both(z_four, 1))
-    flush()
+    flush(early)
     factor_block(3)
 
     ii = lax.broadcasted_iota(jnp.int32, (512, 512), 0)

time: 131 us -> 129 us (0.985)
  Pallas kernels: 131 us -> 128 us
    pallas_call x1, Pallas kernels: 117 us -> 114 us  [body(): pl.pallas_call(fused, out_shape=(shape((512, 2048), bf16), shape((512, 20...]
where the time goes in v4:
time: 129 us; the launch traced here: 128 us
  Pallas kernels  128 us (99%)
    pallas_call x1, Pallas kernels, body(): pl.pallas_call(fused, out_shape=(shape((512, 2048), bf16), shape((512, 20...  114 us
    pallas_call x1, Pallas kernels, body(): pl.pallas_call(finish, grid=(2,), out_shape=(shape((768, 2048), f32), sha...  13.8 us

profile of v4, /device:TPU:1, one launch (start us, length us, event | category | flops | bytes accessed | tf_op | source)
XLA Modules:
  0.0 128.5 jit_solution(14010159542503207535)
XLA Ops:
  0.6 114.1 %factorize.1 = (bf16[512,2048]{1,0:T(8,128)(2,1)}, bf16[512,2048]{1,0:T(8,128)(2,1)}, bf16[768,512]{1,0:T(8,128)(2,1)}, bf16[768,512]{1,0:T(8,128)(2,1)}, bf16[768,512]{1,0:T(8,128)(2,1)}, /*index=5*/f32[8,512]{1,0:T(8,128)}) custom-call(s32[96]{0:T(128)} %perm_ref.1, f32[768,2048]{1,0:T(8,128)} %mom.1, bf16[768,2048]{1,0:T(8,128)(2,1)} %grad.1, ...), custom_call_target="tpu_custom_call" | custom-call | tf_op jit(solution)/shard_map/factorize/pallas_call | solution.py:619
  114.7 13.8 %outputs.1 = (f32[768,2048]{1,0:T(8,128)}, f32[2048,512]{1,0:T(8,128)}, f32[768,2048]{1,0:T(8,128)}) custom-call(f32[768,2048]{1,0:T(8,128)} %mom.1, bf16[768,2048]{1,0:T(8,128)(2,1)} %grad.1, bf16[768,512]{1,0:T(8,128)(2,1)} %get-tuple-element.9.ortho, bf16[768,512]{1,0:T(8,128)(2,1)} %get-tuple-element.10.oph, bf16[768,512]{1,0:T(8,128)(2,1)} %get-tuple-element.11.opl, ...), custom_call_target="tpu_custom_call" | custom-call | flops 6442450944 | bytes 31457280 | tf_op jit(solution)/shard_map/outputs/pallas_call | solution.py:654
